TPU v7x, 32 devices: a whole 2x2x4 slice. The times are simulated.
32 devices in a mesh: groups: 2 (over y), section: 16 (over z, x, core).
Axes of the slice: x: 2, y: 2, z: 4, core: 2. Of those that a mesh axis runs over, the one named last changes fastest.
Arguments:
- held: bfloat16 [16, 128, 4096], P('section', 'groups'), parts along dimension 1, may hold values from 0 to 2
- tile_values: bfloat16 [4608, 128, 128], P('section'), may hold values from -0.25 to 0.25
- tile_rows: int32 [4608], P('section'), may hold values from 0 to 255
- tile_cols: int32 [4608], P('section'), may hold values from 0 to 31
- tile_count: int32 [16], P('section'), may hold values from 1 to 288, as said below
- bias: float32 [65536], P('section'), may hold values from -0.5 to -0.2
Outputs:
- settled: bfloat16 [16, 128, 4096], P('section', 'groups'), parts along dimension 1
There are 2 independent parts, one for each index of `groups`. A program takes and returns all parts, laid end to end along the dimension named above; an argument that names none is the same for every part. Nothing has to cross between parts.
Inputs may be any that keep to these rules, and one draw needn't show every extreme that they name: `tile_count`: slots at or after a list's count are ignored; in every draw some list has all 288 slots live. `tile_rows`: pairs of tile row and tile column may repeat within a list; repeated tiles add.
All inputs are finite; a program needn't handle non-finite values.
Results may differ from a plain program's by a relative error of at most 0.0053.
Values may be sent and summed in bfloat16 or wider, within the bound.
A program may use at most 64 MiB of HBM per device.

v0:
```python
import jax
import jax.numpy as jnp
from jax import lax
from jax.sharding import PartitionSpec as P

TILE = 128
NTILES = 256
SPLIT = 8
TICKS = 2
COLT = 32


def swapped(array, axis, bit):
    return lax.ppermute(array, axis, [(i, i ^ 1 << bit) for i in range(lax.axis_size(axis))])


def from_behind(array, axis, by):
    peers = lax.axis_size(axis)
    return lax.ppermute(array, axis, [(i, (i + by) % peers) for i in range(peers)])


def layer_slab(full_input, rows_list, cols_list, live_count, values_list, bias_slab):
    batch_rows = full_input.shape[0]
    slots = rows_list.shape[0]
    blocks = full_input.reshape(batch_rows, NTILES, TILE)
    live = jnp.arange(slots, dtype=jnp.int32) < live_count
    picked = jnp.take(blocks, rows_list, axis=1)
    picked = jnp.where(live[None, :, None], picked, jnp.zeros_like(picked))
    products = jnp.einsum("bck,ckj->cbj", picked, values_list, preferred_element_type=jnp.float32)
    summed = jax.ops.segment_sum(products, cols_list, num_segments=COLT)
    summed = summed.transpose(1, 0, 2).reshape(batch_rows, COLT * TILE)
    return jnp.maximum(summed + bias_slab[None, :], 0.0).astype(jnp.bfloat16)


def assemble(slab_part):
    position = lax.axis_index("section") % SPLIT
    joined = slab_part
    for bit_index in range(SPLIT.bit_length() - 1):
        partner = swapped(joined, "section", bit_index)
        upper_half = (position >> bit_index) % 2 == 1
        joined = jnp.where(
            upper_half,
            jnp.concatenate([partner, joined], axis=1),
            jnp.concatenate([joined, partner], axis=1),
        )
    return joined


def on_device(held, tile_values, tile_rows, tile_cols, tile_count, bias):
    live_count = tile_count[0]
    full_input = assemble(held[0])
    result = held[0]
    for tick_index in range(TICKS):
        result = layer_slab(full_input, tile_rows, tile_cols, live_count, tile_values, bias)
        if tick_index + 1 < TICKS:
            whole_output = assemble(result)
            full_input = from_behind(whole_output, "section", SPLIT)
    return result[None]


def solution(mesh):
    return jax.shard_map(
        on_device,
        mesh=mesh,
        in_specs=(
            P("section", "groups", None),
            P("section", None, None),
            P("section"),
            P("section"),
            P("section"),
            P("section"),
        ),
        out_specs=P("section", "groups", None),
        check_vma=False,
    )
```

profile of v0, /device:TPU:1, one launch (start us, length us, event | category | flops | bytes accessed | tf_op | source)
XLA Modules:
  0.0 439.4 jit_solution(5128049430844454706)
XLA Ops:
  0.0 0.0 copy-start
  0.0 0.1 collective-permute-start
  0.1 0.0 copy-start.3
  0.1 2.1 collective-permute-done
  2.1 1.5 maximum_select_fusion.5
  3.6 2.4 collective-permute-start.1
  6.0 23.2 %collective-permute-done.1 = bf16[64,8192]{1,0:T(8,128)(2,1)S(1)} collective-permute-done((bf16[64,8192]{1,0:T(8,128)(2,1)S(1)}, bf16[64,8192]{1,0:T(8,128)(2,1)S(1)}, u32[]{:S(2)}, u32[]{:S(2)}) %collective-permute-start.1) | collective-permute-done | bytes 1048608 | tf_op jit(solution)/shard_map/ppermute | solution.py:14
  29.2 1.8 maximum_select_fusion.2
  31.1 1.2 collective-permute-start.2
  32.3 0.0 copy-done
  32.3 0.1 copy.23
  32.4 0.2 copy.8
  33.3 0.0 copy-done.3
  33.3 0.1 copy_bitcast_fusion.3
  33.4 0.2 maximum_select_fusion.6
  33.6 0.3 copy_bitcast_fusion.2
  33.9 0.3 maximum_select_fusion.3
  34.2 43.4 %collective-permute-done.2 = bf16[64,16384]{1,0:T(8,128)(2,1)} collective-permute-done((bf16[64,16384]{1,0:T(8,128)(2,1)}, bf16[64,16384]{1,0:T(8,128)(2,1)}, u32[]{:S(2)}, u32[]{:S(2)}) %collective-permute-start.2) | collective-permute-done | bytes 2097184 | tf_op jit(solution)/shard_map/ppermute | solution.py:14
  77.6 2.2 copy_bitcast_fusion.1
  79.8 2.6 maximum_select_fusion
  82.4 5.7 %gather_fusion = bf16[288,64,128]{2,1,0:T(8,128)(2,1)} fusion(bf16[64,256,128]{2,0,1:T(8,128)(2,1)} %maximum_select_fusion, s32[1024]{0:T(1024)S(1)} %pad_clamp_fusion), kind=kCustom, calls=%fused_computation.clone | custom fusion | bytes 9438336 | tf_op jit(solution)/shard_map/jit(_take)/gather | solution.py:27
  88.2 0.0 copy-start.2
  88.2 11.4 %fusion.1 = f32[288,64,128]{2,1,0:T(8,128)} fusion(bf16[288,128,128]{2,1,0:T(8,128)(2,1)} %param.9, bf16[288,64,128]{2,1,0:T(8,128)(2,1)} %gather_fusion, pred[288]{0:T(512)(128)(4,1)S(1)} %get-tuple-element.7, pred[288]{0:T(512)(128)(4,1)S(1)} %get-tuple-element.6), kind=kOutput, calls=%fused_computation.7 | convolution fusion | flops 608698368 | bytes 23593536 | tf_op jit(solution)/shard_map/bck,ckj->cbj/dot_general | solution.py:29
  99.6 0.1 broadcast.56.clone
  99.7 0.0 copy-done.2
  99.7 0.0 copy-start.1
  99.7 29.8 %scatter_fusion = f32[32,64,128]{2,1,0:T(8,128)S(1)} fusion(f32[32,64,128]{2,1,0:T(8,128)S(1)} %broadcast.56.clone, s32[288]{0:T(512)S(1)} %copy-done.2, f32[288,64,128]{2,1,0:T(8,128)} %fusion.1), kind=kCustom, calls=%fused_computation.2 | custom fusion | flops 2359296 | bytes 28312704 | tf_op jit(solution)/shard_map/scatter-add | solution.py:30
  129.5 0.0 copy-done.1
  129.5 0.1 fusion.13
  129.6 1.9 collective-permute-start.3
  131.5 1.5 collective-permute-done.3
  133.0 0.2 maximum_select_fusion.7
  133.3 1.2 collective-permute-start.4
  134.5 23.2 %collective-permute-done.4 = bf16[64,8192]{1,0:T(8,128)(2,1)S(1)} collective-permute-done((bf16[64,8192]{1,0:T(8,128)(2,1)S(1)}, bf16[64,8192]{1,0:T(8,128)(2,1)S(1)}, u32[]{:S(2)}, u32[]{:S(2)}) %collective-permute-start.4) | collective-permute-done | bytes 1048608 | tf_op jit(solution)/shard_map/ppermute | solution.py:14
  157.7 0.5 maximum_select_fusion.4
  158.2 1.3 collective-permute-start.5
  159.5 44.7 %collective-permute-done.5 = bf16[64,16384]{1,0:T(8,128)(2,1)S(1)} collective-permute-done((bf16[64,16384]{1,0:T(8,128)(2,1)S(1)}, bf16[64,16384]{1,0:T(8,128)(2,1)S(1)}, u32[]{:S(2)}, u32[]{:S(2)}) %collective-permute-start.5) | collective-permute-done | bytes 2097184 | tf_op jit(solution)/shard_map/ppermute | solution.py:14
  204.2 1.0 maximum_select_fusion.1
  205.2 2.3 collective-permute-start.6
  207.5 180.1 %collective-permute-done.6 = bf16[64,32768]{1,0:T(8,128)(2,1)S(1)} collective-permute-done((bf16[64,32768]{1,0:T(8,128)(2,1)S(1)}, bf16[64,32768]{1,0:T(8,128)(2,1)S(1)}, u32[]{:S(2)}, u32[]{:S(2)}) %collective-permute-start.6) | collective-permute-done | bytes 4194336 | tf_op jit(solution)/shard_map/ppermute | solution.py:19
  387.5 3.2 copy_bitcast_fusion
  390.7 5.7 %gather_fusion.1 = bf16[288,64,128]{2,1,0:T(8,128)(2,1)} fusion(bf16[64,256,128]{2,0,1:T(8,128)(2,1)} %copy_bitcast_fusion, s32[1024]{0:T(1024)S(1)} %pad_clamp_fusion), kind=kCustom, calls=%fused_computation.1.clone | custom fusion | bytes 9438336 | tf_op jit(solution)/shard_map/jit(_take)/gather | solution.py:27
  396.4 11.4 %fusion = f32[288,64,128]{2,1,0:T(8,128)} fusion(bf16[288,128,128]{2,1,0:T(8,128)(2,1)} %param.9, bf16[288,64,128]{2,1,0:T(8,128)(2,1)} %gather_fusion.1, pred[288]{0:T(512)(128)(4,1)S(1)} %get-tuple-element.7, pred[288]{0:T(512)(128)(4,1)S(1)} %get-tuple-element.6), kind=kOutput, calls=%fused_computation.5 | convolution fusion | flops 608698368 | bytes 23593536 | tf_op jit(solution)/shard_map/bck,ckj->cbj/dot_general | solution.py:29
  407.8 0.1 broadcast.56
  407.9 29.8 %scatter_fusion.1 = f32[32,64,128]{2,1,0:T(8,128)S(1)} fusion(f32[32,64,128]{2,1,0:T(8,128)S(1)} %broadcast.56, s32[288]{0:T(512)S(1)} %copy-done.2, f32[288,64,128]{2,1,0:T(8,128)} %fusion), kind=kCustom, calls=%fused_computation.3 | custom fusion | flops 2359296 | bytes 28312704 | tf_op jit(solution)/shard_map/scatter-add | solution.py:30
  437.7 0.6 copy.17
  438.4 0.2 reshape.72
  438.6 0.9 maximum_convert_fusion
  (3 shorter events, 0.0 us)
Async XLA Ops:
  0.0 32.3 %copy-start = (bf16[1,64,4096]{2,1,0:T(8,128)(2,1)S(1)}, bf16[1,64,4096]{2,1,0:T(8,128)(2,1)}, u32[]{:S(2)}) copy-start(bf16[1,64,4096]{2,1,0:T(8,128)(2,1)} %param.8) | copy-start | bytes 1572868
  0.0 2.1 collective-permute-start
  0.1 33.2 %copy-start.3 = (s32[288]{0:T(512)S(1)}, s32[288]{0:T(512)}, u32[]{:S(2)}) copy-start(s32[288]{0:T(512)} %param.10) | copy-start | bytes 3460
  3.6 25.6 %collective-permute-start.1 = (bf16[64,8192]{1,0:T(8,128)(2,1)S(1)}, bf16[64,8192]{1,0:T(8,128)(2,1)S(1)}, u32[]{:S(2)}, u32[]{:S(2)}) collective-permute-start(bf16[64,8192]{1,0:T(8,128)(2,1)S(1)} %maximum_select_fusion.5), channel_id=1, source_target_pairs={{0,2},{1,3},{2,0},{3,1},{4,6},{5,7},{6,4},{7,5},{8,10},{9,11},{10,... | collective-permute-start | bytes 3145736 | tf_op jit(solution)/shard_map/ppermute | solution.py:14
  31.1 46.6 %collective-permute-start.2 = (bf16[64,16384]{1,0:T(8,128)(2,1)}, bf16[64,16384]{1,0:T(8,128)(2,1)}, u32[]{:S(2)}, u32[]{:S(2)}) collective-permute-start(bf16[64,16384]{1,0:T(8,128)(2,1)} %maximum_select_fusion.2), channel_id=1, source_target_pairs={{0,4},{1,5},{2,6},{3,7},{4,0},{5,1},{6,2},{7,3},{8,12},{9,13},{10,... | collective-permute-start | bytes 6291464 | tf_op jit(solution)/shard_map/ppermute | solution.py:14
  88.2 11.5 %copy-start.2 = (s32[288]{0:T(512)S(1)}, s32[288]{0:T(512)}, u32[]{:S(2)}) copy-start(s32[288]{0:T(512)} %param.11) | copy-start | bytes 3460
  99.7 29.8 %copy-start.1 = (f32[4096]{0:T(1024)S(1)}, f32[4096]{0:T(1024)}, u32[]{:S(2)}) copy-start(f32[4096]{0:T(1024)} %param.13) | copy-start | bytes 49156
  129.6 3.4 collective-permute-start.3
  133.3 24.4 %collective-permute-start.4 = (bf16[64,8192]{1,0:T(8,128)(2,1)S(1)}, bf16[64,8192]{1,0:T(8,128)(2,1)S(1)}, u32[]{:S(2)}, u32[]{:S(2)}) collective-permute-start(bf16[64,8192]{1,0:T(8,128)(2,1)S(1)} %maximum_select_fusion.7), channel_id=1, source_target_pairs={{0,2},{1,3},{2,0},{3,1},{4,6},{5,7},{6,4},{7,5},{8,10},{9,11},{10,... | collective-permute-start | bytes 3145736 | tf_op jit(solution)/shard_map/ppermute | solution.py:14
  158.2 46.0 %collective-permute-start.5 = (bf16[64,16384]{1,0:T(8,128)(2,1)S(1)}, bf16[64,16384]{1,0:T(8,128)(2,1)S(1)}, u32[]{:S(2)}, u32[]{:S(2)}) collective-permute-start(bf16[64,16384]{1,0:T(8,128)(2,1)S(1)} %maximum_select_fusion.4), channel_id=1, source_target_pairs={{0,4},{1,5},{2,6},{3,7},{4,0},{5,1},{6,2},{7,3},{8,12},{9,13},{10,... | collective-permute-start | bytes 6291464 | tf_op jit(solution)/shard_map/ppermute | solution.py:14
  205.2 182.3 %collective-permute-start.6 = (bf16[64,32768]{1,0:T(8,128)(2,1)S(1)}, bf16[64,32768]{1,0:T(8,128)(2,1)S(1)}, u32[]{:S(2)}, u32[]{:S(2)}) collective-permute-start(bf16[64,32768]{1,0:T(8,128)(2,1)S(1)} %maximum_select_fusion.1), channel_id=1, source_target_pairs={{0,8},{1,9},{2,10},{3,11},{4,12},{5,13},{6,14},{7,15},{8,0},{9,1},... | collective-permute-start | bytes 12582920 | tf_op jit(solution)/shard_map/ppermute | solution.py:19
where the time goes:
time: 443 us; the launch traced here: 439 us
  waiting for transfers between devices  318 us (72%)
  other arithmetic  68.7 us (16%)
  matrix products  22.8 us (5%)
  local copies, waits for them, and re-layouts  18.6 us (4%)
  starting transfers between devices  10.3 us (2%)
    ppermute x1, waiting for transfers between devices, from_behind(): lax.ppermute(array, axis, [(i, (i + by) % peers) for i in range(peers)])  180 us
    ppermute x6, waiting for transfers between devices, swapped(): lax.ppermute(array, axis, [(i, i ^ 1 << bit) for i in range(lax.axis_size...  138 us
    scatter-add x2, other arithmetic, layer_slab(): summed = jax.ops.segment_sum(products, cols_list, num_segments=COLT)  59.6 us
    dot_general x2, matrix products, layer_slab(): jnp.einsum('bck,ckj->cbj', picked, values_list, preferred_element_type=jn...  22.8 us
    gather x2, local copies, waits for them, and re-layouts, layer_slab(): picked = jnp.take(blocks, rows_list, axis=1)  11.5 us
  transfers between devices with their start and end apart: 7, of which 7 were waited for; matrix products, arithmetic and copies ran while one was open for 0% of the time, Pallas kernels for 0%

commit v1 on v0

v1 whole, which is shorter than its diff:
```python
import functools

import jax
import jax.numpy as jnp
from jax import lax
from jax.experimental import pallas as pl
from jax.experimental.pallas import tpu as pltpu
from jax.sharding import PartitionSpec as P

TILE = 128
SPLIT = 8
COLT = 32
HALVES = 2
PIECES = 2
PIECE = COLT // PIECES
GROUP = 8
WPARTS = 4
SIB, XN, ZN = 1, 2, 4
N_SENDS = HALVES * (14 + 16)


def kernel(peers, rows_ref, prev_ref, last_ref, held_ref, w_hbm, bias_ref, out_ref,
           xa0, xa1, xb0, xb1, y0, y1, w, buf, wsem, send_sem, recv_sem):
    xs = ((xa0, xa1), (xb0, xb1))
    ys = (y0, y1)
    slots = rows_ref.shape[0]
    part = held_ref.shape[1] // HALVES
    me = lax.axis_index("section")
    place = me % SPLIT
    base = me - place
    bits = (place % 2, (place // 2) % 2, place // 4)
    nxt = (me + SPLIT) % peers
    prv = (me + peers - SPLIT) % peers

    def moved(rel):
        at = place
        for b in range(3):
            if rel >> b & 1:
                at = at + (1 - 2 * bits[b]) * (1 << b)
        return at

    def slab(x, rel, k):
        return x.at[pl.ds(moved(rel) * COLT + k * PIECE, PIECE)]

    wsize = slots // WPARTS
    wcopies = [
        pltpu.make_async_copy(
            w_hbm.at[pl.ds(i * wsize, wsize)], w.at[pl.ds(i * wsize, wsize)], wsem.at[i])
        for i in range(WPARTS)
    ]
    for c in wcopies:
        c.start()

    barrier = pltpu.get_barrier_semaphore()
    for dev in (base + moved(SIB), base + moved(XN), base + moved(ZN), nxt, prv):
        pl.semaphore_signal(barrier, inc=1, device_id={"section": dev},
                            device_id_type=pl.DeviceIdType.MESH)

    for h in range(HALVES):
        for c in range(COLT):
            xs[0][h][place * COLT + c] = held_ref[0, h * part:(h + 1) * part, c * TILE:(c + 1) * TILE]
    buf[slots] = jnp.zeros(buf.shape[1:], buf.dtype)
    pl.semaphore_wait(barrier, 5)

    sent = []

    def send(t, h, rel, k, hop):
        x = xs[t][h]
        copy = pltpu.make_async_remote_copy(
            src_ref=slab(x, rel, k), dst_ref=slab(x, rel, k),
            send_sem=send_sem.at[len(sent)], recv_sem=recv_sem.at[t, h, rel ^ hop, k],
            device_id={"section": base + moved(hop)}, device_id_type=pl.DeviceIdType.MESH)
        copy.start()
        sent.append(copy)

    def send_next(h, k):
        copy = pltpu.make_async_remote_copy(
            src_ref=ys[h].at[pl.ds(k * PIECE, PIECE)], dst_ref=slab(xs[1][h], 0, k),
            send_sem=send_sem.at[len(sent)], recv_sem=recv_sem.at[1, h, 0, k],
            device_id={"section": nxt}, device_id_type=pl.DeviceIdType.MESH)
        copy.start()
        sent.append(copy)

    def arrive(t, h, rel, k):
        x = xs[t][h]
        pltpu.make_async_remote_copy(
            src_ref=slab(x, rel, k), dst_ref=slab(x, rel, k),
            send_sem=send_sem.at[0], recv_sem=recv_sem.at[t, h, rel, k],
            device_id={"section": base + moved(SIB)},
            device_id_type=pl.DeviceIdType.MESH).wait_recv()

    def step(t, h, rel, k, hops):
        def run():
            arrive(t, h, rel, k)
            for hop in hops:
                send(t, h, rel, k, hop)
        return run

    def own(h):
        for k in range(PIECES):
            send(0, h, 0, k, ZN)
            send(0, h, 0, PIECES - 1 - k, XN)
        for k in range(PIECES):
            send(0, h, 0, k, SIB)

    def gather_steps(h):
        return [
            step(0, h, ZN, 0, (XN, SIB)),
            step(0, h, XN, 1, (ZN, SIB)),
            step(0, h, ZN, 1, (SIB,)),
            step(0, h, XN, 0, (SIB,)),
            step(0, h, XN + ZN, 0, (SIB,)),
            step(0, h, XN + ZN, 1, (SIB,)),
        ]

    def pass_steps(h):
        every = []
        for rel, hops in ((0, (ZN, XN, SIB)), (ZN, (XN, SIB)), (XN, (SIB,)), (XN + ZN, (SIB,))):
            every += [step(1, h, rel, k, hops) for k in range(PIECES)]
        return every

    def settle(t, h):
        for rel in (1, 3, 5, 7):
            for k in range(PIECES):
                arrive(t, h, rel, k)

    def tiles(x, low, high):
        def body(i, carry):
            done = []
            for j in range(GROUP):
                s = i * GROUP + j
                done.append(jnp.dot(x[rows_ref[s]], w[s], preferred_element_type=jnp.float32))
            for j in range(GROUP):
                s = i * GROUP + j
                buf[s] = done[j] + buf[prev_ref[s]]
            return carry
        lax.fori_loop(low, high, body, 0)

    def layer(t, h, steps, segments, first):
        groups = slots // GROUP
        edges = [groups * i // segments for i in range(segments + 1)]
        steps = list(steps)
        for i in range(segments):
            tiles(xs[t][h], edges[i], edges[i + 1])
            if i >= first and steps:
                steps.pop(0)()
        for run in steps:
            run()
        for c in range(COLT):
            value = jnp.maximum(buf[last_ref[c]] + bias_ref[c:c + 1, :], 0.0).astype(jnp.bfloat16)
            if t == 0:
                ys[h][c] = value
                if (c + 1) % PIECE == 0:
                    send_next(h, c // PIECE)
            else:
                out_ref[0, h * part:(h + 1) * part, c * TILE:(c + 1) * TILE] = value

    own(0)
    early = gather_steps(0)
    for run in early[:2]:
        run()
    own(1)
    for run in early[2:]:
        run()
    settle(0, 0)
    for c in wcopies:
        c.wait()
    layer(0, 0, gather_steps(1), 7, 0)
    settle(0, 1)
    first_pass = pass_steps(0)
    layer(0, 1, first_pass[:1], 4, 2)
    for run in first_pass[1:]:
        run()
    settle(1, 0)
    layer(1, 0, pass_steps(1), 9, 0)
    settle(1, 1)
    layer(1, 1, (), 1, 0)
    for copy in sent:
        copy.wait_send()


def links(cols, live_count):
    slots = cols.shape[0]
    at = jnp.arange(slots, dtype=jnp.int32)
    same = (cols[:, None] == cols[None, :]) & (at[None, :] < at[:, None])
    prev = jnp.max(jnp.where(same, at[None, :], -1), axis=1)
    mine = (cols[None, :] == jnp.arange(COLT, dtype=jnp.int32)[:, None]) & (at < live_count)[None, :]
    last = jnp.max(jnp.where(mine, at[None, :], -1), axis=1)
    return jnp.where(prev < 0, slots, prev), jnp.where(last < 0, slots, last)


def on_device(peers, held, tile_values, tile_rows, tile_cols, tile_count, bias):
    slots = tile_rows.shape[0]
    batch = held.shape[1]
    part = batch // HALVES
    prev, last = links(tile_cols, tile_count[0])
    smem = pl.BlockSpec(memory_space=pltpu.SMEM)
    vmem = pl.BlockSpec(memory_space=pltpu.VMEM)
    x = pltpu.VMEM((SPLIT * COLT, part, TILE), jnp.bfloat16)
    y = pltpu.VMEM((COLT, part, TILE), jnp.bfloat16)
    return pl.pallas_call(
        functools.partial(kernel, peers),
        out_shape=jax.ShapeDtypeStruct(held.shape, jnp.bfloat16),
        in_specs=[smem, smem, smem, vmem, pl.BlockSpec(memory_space=pl.ANY), vmem],
        out_specs=vmem,
        scratch_shapes=[
            x, x, x, x, y, y,
            pltpu.VMEM((slots, TILE, TILE), jnp.bfloat16),
            pltpu.VMEM((slots + 1, part, TILE), jnp.float32),
            pltpu.SemaphoreType.DMA((WPARTS,)),
            pltpu.SemaphoreType.DMA((N_SENDS,)),
            pltpu.SemaphoreType.DMA((2, HALVES, SPLIT, PIECES)),
        ],
        compiler_params=pltpu.CompilerParams(
            collective_id=0, has_side_effects=True, vmem_limit_bytes=56 * 1024 * 1024),
    )(tile_rows, prev, last, held, tile_values, bias.reshape(COLT, TILE))


def solution(mesh):
    return jax.shard_map(
        functools.partial(on_device, mesh.shape["section"]),
        mesh=mesh,
        in_specs=(
            P("section", "groups", None),
            P("section", None, None),
            P("section"),
            P("section"),
            P("section"),
            P("section"),
        ),
        out_specs=P("section", "groups", None),
        check_vma=False,
    )
```

time: 443 us -> 84 us (0.19)
  waiting for transfers between devices: 318 us -> 0 us
  Pallas kernels: 0 us -> 78.2 us
  other arithmetic: 68.7 us -> 2.98 us
  matrix products: 22.8 us -> 0 us
  local copies, waits for them, and re-layouts: 18.6 us -> 1.87 us
  starting transfers between devices: 10.3 us -> 0 us
    ppermute x7 -> x0, waiting for transfers between devices: 318 us -> none  [the longest x1 180 us: from_behind(): lax.ppermute(array, axis, [(i, (i + by) % peers) for i in range(peers)])]
    pallas_call x0 -> x1, Pallas kernels: none -> 78.2 us  [on_device(): pl.pallas_call(functools.partial(kernel, peers), out_shape=jax.ShapeDtype...]
    scatter-add x2 -> x0, other arithmetic: 59.6 us -> none  [layer_slab(): summed = jax.ops.segment_sum(products, cols_list, num_segments=COLT)]
    dot_general x2 -> x0, matrix products: 22.8 us -> none  [layer_slab(): jnp.einsum('bck,ckj->cbj', picked, values_list, preferred_element_type=jn...]
    gather x2 -> x0, local copies, waits for them, and re-layouts: 11.5 us -> none  [layer_slab(): picked = jnp.take(blocks, rows_list, axis=1)]
    ppermute x7 -> x0, starting transfers between devices: 10.3 us -> none  [the longest x6 8.03 us: swapped(): lax.ppermute(array, axis, [(i, i ^ 1 << bit) for i in range(lax.axis_size...]
    select_n x9 -> x2, other arithmetic: 8.1 us -> 1.19 us  [links(): return (jnp.where(prev < 0, slots, prev), jnp.where(last < 0, slots, last))]
  transfers between devices with their start and end apart: 7 -> 0, of which waited for: 7 -> 0; matrix products, arithmetic and copies ran while one was open for 0% -> 0% of each run, Pallas kernels for 0% -> 0%
where the time goes in v1:
time: 84 us; the launch traced here: 83.7 us
  Pallas kernels  78.2 us (93%)
  other arithmetic  2.98 us (4%)
  local copies, waits for them, and re-layouts  1.87 us (2%)
    pallas_call x1, Pallas kernels, on_device(): pl.pallas_call(functools.partial(kernel, peers), out_shape=jax.ShapeDtype...  78.2 us
    unnamed x1, local copies, waits for them, and re-layouts  1.87 us

profile of v1, /device:TPU:1, one launch (start us, length us, event | category | flops | bytes accessed | tf_op | source)
XLA Modules:
  0.0 83.7 jit_solution(12568206209504182135)
XLA Ops:
  0.7 0.8 select_reduce_fusion.1
  1.5 0.6 compare_select_fusion.1.last_ref
  2.1 1.0 %select_reduce_fusion = s32[288]{0:T(512)S(1)} fusion(s32[288]{0:T(512)} %param.9), kind=kLoop, calls=%fused_computation | loop fusion | flops 414432 | bytes 2304 | tf_op jit(solution)/shard_map/reduce_max | solution.py:186
  3.1 0.6 compare_select_fusion.prev_ref
  3.6 78.2 %shard_map.64 = bf16[1,64,4096]{2,1,0:T(8,128)(2,1)} custom-call(s32[288]{0:T(512)} %rows_ref.1, s32[288]{0:T(512)} %compare_select_fusion.prev_ref, s32[32]{0:T(128)} %compare_select_fusion.1.last_ref, bf16[1,64,4096]{2,1,0:T(8,128)(2,1)} %held_ref.1, bf16[288,128,128]{2,1,0:T(8,128)(2,1)} %w_hbm.1, f32[32,128]{1,0:T(8,128)} %bitcast.3), custom_call_target="tpu_custom_call" | custom-call | tf_op jit(solution)/shard_map/pallas_call | solution.py:201
  81.8 1.9 %copy.9 = bf16[1,64,4096]{2,1,0:T(8,128)(2,1)} copy(bf16[1,64,4096]{2,1,0:T(8,128)(2,1)} %shard_map.64) | data formatting | bytes 1048576
  (1 shorter events, 0.0 us)

commit v2 on v1

--- a/solution.py
+++ b/solution.py
@@ -13,17 +13,63 @@
 HALVES = 2
 PIECES = 2
 PIECE = COLT // PIECES
-GROUP = 8
+GROUP = 40
+LANES = 384
 WPARTS = 4
 SIB, XN, ZN = 1, 2, 4
 N_SENDS = HALVES * (14 + 16)
 
 
-def kernel(peers, rows_ref, prev_ref, last_ref, held_ref, w_hbm, bias_ref, out_ref,
-           xa0, xa1, xb0, xb1, y0, y1, w, buf, wsem, send_sem, recv_sem):
+def order(rows, cols, count):
+    slots = cols.shape[1]
+    pairs = (slots + COLT) // 2
+
+    def iota(shape, axis):
+        return lax.broadcasted_iota(jnp.int32, shape, axis)
+
+    def total(mask, value, axis):
+        return jnp.sum(jnp.where(mask, value, 0), axis=axis, keepdims=True)
+
+    square = (slots, slots)
+    diagonal = iota(square, 0) == iota(square, 1)
+
+    def upright(line):
+        return total(diagonal, line, 1)
+
+    key = jnp.where(iota((1, slots), 1) < count, cols, COLT)
+    key_up = upright(key)
+    rank = total((key_up == key) & (iota(square, 0) < iota(square, 1)), 1, 0)
+    below = total(key_up < key, 1, 0)
+    column_up = iota((COLT, slots), 0)
+    held_by = total(column_up == key, 1, 1)
+    odd = held_by & 1
+    pads = total(column_up < key, odd, 0)
+    position = jnp.where(key < COLT, below + pads + rank, -1)
+
+    wide = (slots, LANES)
+    here = upright(position) == iota(wide, 1)
+    zero_row = SPLIT * COLT
+    slot = total(here, iota(wide, 0), 0)
+    row = zero_row + total(here, upright(rows) - zero_row, 0)
+    opens = total(here & (upright(rank) == 0), 1, 0)
+
+    column = iota((COLT, LANES), 1)
+    column_up = iota((COLT, LANES), 0)
+    upto = total(column_up <= column, held_by + odd, 0)
+    mine = total(column_up == column, held_by, 0)
+    closes = jnp.where(mine > 0, (upto >> 1) - 1, pairs)
+    slot = jnp.clip(slot, 0, slots - 1)
+    row = jnp.clip(row, 0, zero_row)
+    closes = jnp.clip(closes, 0, pairs)
+    return jnp.concatenate([slot, row, opens, closes, jnp.zeros((4, LANES), jnp.int32)], axis=0)
+
+
+def kernel(peers, count_ref, rows_ref, cols_ref, held_ref, w_hbm, bias_ref, out_ref,
+           xa0, xa1, xb0, xb1, y0, y1, w, buf, plan, plan_ref, wsem, psem, send_sem, recv_sem):
     xs = ((xa0, xa1), (xb0, xb1))
     ys = (y0, y1)
-    slots = rows_ref.shape[0]
+    slots = rows_ref.shape[1]
+    pairs = (slots + COLT) // 2
     part = held_ref.shape[1] // HALVES
     me = lax.axis_index("section")
     place = me % SPLIT
@@ -59,7 +105,9 @@
     for h in range(HALVES):
         for c in range(COLT):
             xs[0][h][place * COLT + c] = held_ref[0, h * part:(h + 1) * part, c * TILE:(c + 1) * TILE]
-    buf[slots] = jnp.zeros(buf.shape[1:], buf.dtype)
+    buf[pairs] = jnp.zeros(buf.shape[1:], buf.dtype)
+    for x in xs[0] + xs[1]:
+        x[SPLIT * COLT] = jnp.zeros(x.shape[1:], x.dtype)
     pl.semaphore_wait(barrier, 5)
 
     sent = []
@@ -124,30 +172,35 @@
             for k in range(PIECES):
                 arrive(t, h, rel, k)
 
-    def tiles(x, low, high):
-        def body(i, carry):
-            done = []
+    def tiles(x, low, high, total):
+        def body(i, total):
             for j in range(GROUP):
-                s = i * GROUP + j
-                done.append(jnp.dot(x[rows_ref[s]], w[s], preferred_element_type=jnp.float32))
-            for j in range(GROUP):
-                s = i * GROUP + j
-                buf[s] = done[j] + buf[prev_ref[s]]
-            return carry
-        lax.fori_loop(low, high, body, 0)
+                pair = i * GROUP + j
+                a, b = 2 * pair, 2 * pair + 1
+                left = jnp.concatenate([x[plan_ref[1, a]], x[plan_ref[1, b]]], axis=1)
+                right = jnp.concatenate([w[plan_ref[0, a]], w[plan_ref[0, b]]], axis=0)
+                product = jnp.dot(left, right, preferred_element_type=jnp.float32)
+                total = jnp.where(plan_ref[2, a] == 1, product, total + product)
+                buf[pair] = total
+            return total
+        return lax.fori_loop(low, high, body, total)
 
     def layer(t, h, steps, segments, first):
-        groups = slots // GROUP
+        groups = pairs // GROUP
         edges = [groups * i // segments for i in range(segments + 1)]
         steps = list(steps)
+        each = -(-len(steps) // max(1, segments - first))
+        total = jnp.zeros(buf.shape[1:], buf.dtype)
         for i in range(segments):
-            tiles(xs[t][h], edges[i], edges[i + 1])
-            if i >= first and steps:
-                steps.pop(0)()
+            total = tiles(xs[t][h], edges[i], edges[i + 1], total)
+            if i >= first:
+                for run in steps[:each]:
+                    run()
+                steps = steps[each:]
         for run in steps:
             run()
         for c in range(COLT):
-            value = jnp.maximum(buf[last_ref[c]] + bias_ref[c:c + 1, :], 0.0).astype(jnp.bfloat16)
+            value = jnp.maximum(buf[plan_ref[3, c]] + bias_ref[c:c + 1, :], 0.0).astype(jnp.bfloat16)
             if t == 0:
                 ys[h][c] = value
                 if (c + 1) % PIECE == 0:
@@ -156,6 +209,9 @@
                 out_ref[0, h * part:(h + 1) * part, c * TILE:(c + 1) * TILE] = value
 
     own(0)
+    plan[...] = order(rows_ref[...], cols_ref[...], count_ref[0])
+    plan_copy = pltpu.make_async_copy(plan, plan_ref, psem)
+    plan_copy.start()
     early = gather_steps(0)
     for run in early[:2]:
         run()
@@ -163,57 +219,51 @@
     for run in early[2:]:
         run()
     settle(0, 0)
+    plan_copy.wait()
     for c in wcopies:
         c.wait()
-    layer(0, 0, gather_steps(1), 7, 0)
+    layer(0, 0, gather_steps(1), 4, 0)
     settle(0, 1)
     first_pass = pass_steps(0)
     layer(0, 1, first_pass[:1], 4, 2)
     for run in first_pass[1:]:
         run()
     settle(1, 0)
-    layer(1, 0, pass_steps(1), 9, 0)
+    layer(1, 0, pass_steps(1), 4, 0)
     settle(1, 1)
     layer(1, 1, (), 1, 0)
     for copy in sent:
         copy.wait_send()
 
 
-def links(cols, live_count):
-    slots = cols.shape[0]
-    at = jnp.arange(slots, dtype=jnp.int32)
-    same = (cols[:, None] == cols[None, :]) & (at[None, :] < at[:, None])
-    prev = jnp.max(jnp.where(same, at[None, :], -1), axis=1)
-    mine = (cols[None, :] == jnp.arange(COLT, dtype=jnp.int32)[:, None]) & (at < live_count)[None, :]
-    last = jnp.max(jnp.where(mine, at[None, :], -1), axis=1)
-    return jnp.where(prev < 0, slots, prev), jnp.where(last < 0, slots, last)
-
-
 def on_device(peers, held, tile_values, tile_rows, tile_cols, tile_count, bias):
     slots = tile_rows.shape[0]
     batch = held.shape[1]
     part = batch // HALVES
-    prev, last = links(tile_cols, tile_count[0])
+    pairs = (slots + COLT) // 2
     smem = pl.BlockSpec(memory_space=pltpu.SMEM)
     vmem = pl.BlockSpec(memory_space=pltpu.VMEM)
-    x = pltpu.VMEM((SPLIT * COLT, part, TILE), jnp.bfloat16)
+    x = pltpu.VMEM((SPLIT * COLT + 1, part, TILE), jnp.bfloat16)
     y = pltpu.VMEM((COLT, part, TILE), jnp.bfloat16)
     return pl.pallas_call(
         functools.partial(kernel, peers),
         out_shape=jax.ShapeDtypeStruct(held.shape, jnp.bfloat16),
-        in_specs=[smem, smem, smem, vmem, pl.BlockSpec(memory_space=pl.ANY), vmem],
+        in_specs=[smem, vmem, vmem, vmem, pl.BlockSpec(memory_space=pl.ANY), vmem],
         out_specs=vmem,
         scratch_shapes=[
             x, x, x, x, y, y,
             pltpu.VMEM((slots, TILE, TILE), jnp.bfloat16),
-            pltpu.VMEM((slots + 1, part, TILE), jnp.float32),
+            pltpu.VMEM((pairs + 1, part, TILE), jnp.float32),
+            pltpu.VMEM((8, LANES), jnp.int32),
+            pltpu.SMEM((8, LANES), jnp.int32),
             pltpu.SemaphoreType.DMA((WPARTS,)),
+            pltpu.SemaphoreType.DMA,
             pltpu.SemaphoreType.DMA((N_SENDS,)),
             pltpu.SemaphoreType.DMA((2, HALVES, SPLIT, PIECES)),
         ],
         compiler_params=pltpu.CompilerParams(
             collective_id=0, has_side_effects=True, vmem_limit_bytes=56 * 1024 * 1024),
-    )(tile_rows, prev, last, held, tile_values, bias.reshape(COLT, TILE))
+    )(tile_count, tile_rows.reshape(1, slots), tile_cols.reshape(1, slots), held, tile_values, bias.reshape(COLT, TILE))
 
 
 def solution(mesh):

time: 84 us -> 75.5 us (0.90)
  Pallas kernels: 78.2 us -> 70.2 us
  other arithmetic: 2.98 us -> 0 us
  local copies, waits for them, and re-layouts: 1.87 us -> 4.39 us
    pallas_call x1, Pallas kernels: 78.2 us -> 70.2 us  [on_device(): pl.pallas_call(functools.partial(kernel, peers), out_shape=jax.ShapeDtype...]
    reshape x0 -> x2, local copies, waits for them, and re-layouts: none -> 2.52 us  [the longest x1 1.27 us: on_device(): tile_cols.reshape(1, slots)]
    reduce_max x2 -> x0, other arithmetic: 1.79 us -> none  [the longest x1 0.98 us: links(): prev = jnp.max(jnp.where(same, at[None, :], -1), axis=1)]
    select_n x2 -> x0, other arithmetic: 1.19 us -> none  [links(): return (jnp.where(prev < 0, slots, prev), jnp.where(last < 0, slots, last))]
where the time goes in v2:
time: 75.5 us; the launch traced here: 75.2 us
  Pallas kernels  70.2 us (93%)
  local copies, waits for them, and re-layouts  4.39 us (6%)
    pallas_call x1, Pallas kernels, on_device(): pl.pallas_call(functools.partial(kernel, peers), out_shape=jax.ShapeDtype...  70.2 us
    unnamed x1, local copies, waits for them, and re-layouts  1.87 us

profile of v2, /device:TPU:1, one launch (start us, length us, event | category | flops | bytes accessed | tf_op | source)
XLA Modules:
  0.0 75.2 jit_solution(5462864329102764052)
XLA Ops:
  0.7 1.2 %reshape.9.rows_ref = s32[1,288]{1,0:T(1,128)} reshape(s32[288]{0:T(512)} %param.8) | data formatting | bytes 2304 | tf_op jit(solution)/shard_map/reshape | solution.py:266
  1.9 1.3 %reshape.10.cols_ref = s32[1,288]{1,0:T(1,128)} reshape(s32[288]{0:T(512)} %param.9) | data formatting | bytes 2304 | tf_op jit(solution)/shard_map/reshape | solution.py:266
  3.2 70.2 %shard_map.64 = bf16[1,64,4096]{2,1,0:T(8,128)(2,1)} custom-call(s32[1]{0:T(128)S(6)} %copy.8.count_ref, s32[1,288]{1,0:T(1,128)} %reshape.9.rows_ref, s32[1,288]{1,0:T(1,128)} %reshape.10.cols_ref, bf16[1,64,4096]{2,1,0:T(8,128)(2,1)} %held_ref.1, bf16[288,128,128]{2,1,0:T(8,128)(2,1)} %w_hbm.1, f32[32,128]{1,0:T(8,128)} %bitcast.1), custom_call_target="tpu_custom_call" | custom-call | tf_op jit(solution)/shard_map/pallas_call | solution.py:248
  73.4 1.9 %copy.9 = bf16[1,64,4096]{2,1,0:T(8,128)(2,1)} copy(bf16[1,64,4096]{2,1,0:T(8,128)(2,1)} %shard_map.64) | data formatting | bytes 1048576

commit v3 on v2

--- a/solution.py
+++ b/solution.py
@@ -17,7 +17,7 @@
 LANES = 384
 WPARTS = 4
 SIB, XN, ZN = 1, 2, 4
-N_SENDS = HALVES * (14 + 16)
+N_SENDS = HALVES * PIECES * (7 + 8)
 
 
 def order(rows, cols, count):
@@ -68,7 +68,7 @@
            xa0, xa1, xb0, xb1, y0, y1, w, buf, plan, plan_ref, wsem, psem, send_sem, recv_sem):
     xs = ((xa0, xa1), (xb0, xb1))
     ys = (y0, y1)
-    slots = rows_ref.shape[1]
+    slots = rows_ref.shape[0]
     pairs = (slots + COLT) // 2
     part = held_ref.shape[1] // HALVES
     me = lax.axis_index("section")
@@ -147,24 +147,26 @@
     def own(h):
         for k in range(PIECES):
             send(0, h, 0, k, ZN)
-            send(0, h, 0, PIECES - 1 - k, XN)
+            send(0, h, 0, (k + PIECES // 2) % PIECES, XN)
         for k in range(PIECES):
             send(0, h, 0, k, SIB)
 
     def gather_steps(h):
-        return [
-            step(0, h, ZN, 0, (XN, SIB)),
-            step(0, h, XN, 1, (ZN, SIB)),
-            step(0, h, ZN, 1, (SIB,)),
-            step(0, h, XN, 0, (SIB,)),
-            step(0, h, XN + ZN, 0, (SIB,)),
-            step(0, h, XN + ZN, 1, (SIB,)),
-        ]
+        direct, diagonal = [], []
+        for i in range(PIECES):
+            j = (i + PIECES // 2) % PIECES
+            direct.append(step(0, h, ZN, i, (XN, SIB) if i < PIECES // 2 else (SIB,)))
+            direct.append(step(0, h, XN, j, (ZN, SIB) if j >= PIECES // 2 else (SIB,)))
+        for i in range(PIECES // 2):
+            diagonal.append(step(0, h, XN + ZN, i, (SIB,)))
+            diagonal.append(step(0, h, XN + ZN, i + PIECES // 2, (SIB,)))
+        return direct + diagonal
 
     def pass_steps(h):
         every = []
-        for rel, hops in ((0, (ZN, XN, SIB)), (ZN, (XN, SIB)), (XN, (SIB,)), (XN + ZN, (SIB,))):
-            every += [step(1, h, rel, k, hops) for k in range(PIECES)]
+        for k in range(PIECES):
+            for rel, hops in ((0, (ZN, XN, SIB)), (ZN, (XN, SIB)), (XN, (SIB,)), (XN + ZN, (SIB,))):
+                every.append(step(1, h, rel, k, hops))
         return every
 
     def settle(t, h):
@@ -185,20 +187,12 @@
             return total
         return lax.fori_loop(low, high, body, total)
 
-    def layer(t, h, steps, segments, first):
-        groups = pairs // GROUP
-        edges = [groups * i // segments for i in range(segments + 1)]
-        steps = list(steps)
-        each = -(-len(steps) // max(1, segments - first))
+    def layer(t, h, between):
         total = jnp.zeros(buf.shape[1:], buf.dtype)
-        for i in range(segments):
-            total = tiles(xs[t][h], edges[i], edges[i + 1], total)
-            if i >= first:
-                for run in steps[:each]:
-                    run()
-                steps = steps[each:]
-        for run in steps:
-            run()
+        for i in range(pairs // GROUP):
+            total = tiles(xs[t][h], i, i + 1, total)
+            for run in between.get(i, ()):
+                run()
         for c in range(COLT):
             value = jnp.maximum(buf[plan_ref[3, c]] + bias_ref[c:c + 1, :], 0.0).astype(jnp.bfloat16)
             if t == 0:
@@ -209,29 +203,36 @@
                 out_ref[0, h * part:(h + 1) * part, c * TILE:(c + 1) * TILE] = value
 
     own(0)
-    plan[...] = order(rows_ref[...], cols_ref[...], count_ref[0])
+    plan[...] = order(rows_ref[...][None, :], cols_ref[...][None, :], count_ref[0])
     plan_copy = pltpu.make_async_copy(plan, plan_ref, psem)
     plan_copy.start()
-    early = gather_steps(0)
-    for run in early[:2]:
+    ahead = PIECES
+    first = gather_steps(0)
+    for run in first[:ahead]:
         run()
     own(1)
-    for run in early[2:]:
+    for run in first[ahead:]:
         run()
     settle(0, 0)
     plan_copy.wait()
     for c in wcopies:
         c.wait()
-    layer(0, 0, gather_steps(1), 4, 0)
+    second = gather_steps(1)
+    half = ahead // 2
+    layer(0, 0, {1: second[:half], 2: second[half:ahead]})
+    for run in second[ahead:]:
+        run()
     settle(0, 1)
-    first_pass = pass_steps(0)
-    layer(0, 1, first_pass[:1], 4, 2)
-    for run in first_pass[1:]:
+    layer(0, 1, {})
+    for run in pass_steps(0):
         run()
     settle(1, 0)
-    layer(1, 0, pass_steps(1), 4, 0)
+    final = pass_steps(1)
+    layer(1, 0, {i: final[i:i + 1] for i in range(4)})
+    for run in final[4:]:
+        run()
     settle(1, 1)
-    layer(1, 1, (), 1, 0)
+    layer(1, 1, {})
     for copy in sent:
         copy.wait_send()
 
@@ -263,7 +264,7 @@
         ],
         compiler_params=pltpu.CompilerParams(
             collective_id=0, has_side_effects=True, vmem_limit_bytes=56 * 1024 * 1024),
-    )(tile_count, tile_rows.reshape(1, slots), tile_cols.reshape(1, slots), held, tile_values, bias.reshape(COLT, TILE))
+    )(tile_count, tile_rows, tile_cols, held, tile_values, bias.reshape(COLT, TILE))
 
 
 def solution(mesh):

time: 75.5 us -> 80.6 us (1.068)
  Pallas kernels: 70.2 us -> 77.9 us
  local copies, waits for them, and re-layouts: 4.39 us -> 1.87 us
    pallas_call x1, Pallas kernels: 70.2 us -> 77.9 us  [on_device(): pl.pallas_call(functools.partial(kernel, peers), out_shape=jax.ShapeDtype...]
    reshape x2 -> x0, local copies, waits for them, and re-layouts: 2.52 us -> none  [the longest x1 1.27 us: on_device(): tile_cols.reshape(1, slots)]
where the time goes in v3:
time: 80.6 us; the launch traced here: 80.4 us
  Pallas kernels  77.9 us (97%)
  local copies, waits for them, and re-layouts  1.87 us (2%)
    pallas_call x1, Pallas kernels, on_device(): pl.pallas_call(functools.partial(kernel, peers), out_shape=jax.ShapeDtype...  77.9 us
    unnamed x1, local copies, waits for them, and re-layouts  1.87 us

profile of v3, /device:TPU:1, one launch (start us, length us, event | category | flops | bytes accessed | tf_op | source)
XLA Modules:
  0.0 80.4 jit_solution(8946297494372246006)
XLA Ops:
  0.7 77.9 %shard_map.64 = bf16[1,64,4096]{2,1,0:T(8,128)(2,1)} custom-call(s32[1]{0:T(128)S(6)} %copy.8.count_ref, s32[288]{0:T(512)} %rows_ref.1, s32[288]{0:T(512)} %cols_ref.1, bf16[1,64,4096]{2,1,0:T(8,128)(2,1)} %held_ref.1, bf16[288,128,128]{2,1,0:T(8,128)(2,1)} %w_hbm.1, f32[32,128]{1,0:T(8,128)} %bitcast.1), custom_call_target="tpu_custom_call" | custom-call | tf_op jit(solution)/shard_map/pallas_call | solution.py:249
  78.5 1.9 %copy.9 = bf16[1,64,4096]{2,1,0:T(8,128)(2,1)} copy(bf16[1,64,4096]{2,1,0:T(8,128)(2,1)} %shard_map.64) | data formatting | bytes 1048576

commit v4 on v3

--- a/solution.py
+++ b/solution.py
@@ -110,7 +110,7 @@
         x[SPLIT * COLT] = jnp.zeros(x.shape[1:], x.dtype)
     pl.semaphore_wait(barrier, 5)
 
-    sent = []
+    sent, pushed = [], []
 
     def send(t, h, rel, k, hop):
         x = xs[t][h]
@@ -128,6 +128,12 @@
             device_id={"section": nxt}, device_id_type=pl.DeviceIdType.MESH)
         copy.start()
         sent.append(copy)
+        pushed.append(copy)
+
+    def push(h, k):
+        if pushed:
+            pushed[-1].wait_send()
+        send_next(h, k)
 
     def arrive(t, h, rel, k):
         x = xs[t][h]
@@ -162,12 +168,9 @@
             diagonal.append(step(0, h, XN + ZN, i + PIECES // 2, (SIB,)))
         return direct + diagonal
 
-    def pass_steps(h):
-        every = []
-        for k in range(PIECES):
-            for rel, hops in ((0, (ZN, XN, SIB)), (ZN, (XN, SIB)), (XN, (SIB,)), (XN + ZN, (SIB,))):
-                every.append(step(1, h, rel, k, hops))
-        return every
+    def pass_step(h, rel, k):
+        hops = {0: (ZN, XN, SIB), ZN: (XN, SIB)}.get(rel, (SIB,))
+        return step(1, h, rel, k, hops)
 
     def settle(t, h):
         for rel in (1, 3, 5, 7):
@@ -197,8 +200,6 @@
             value = jnp.maximum(buf[plan_ref[3, c]] + bias_ref[c:c + 1, :], 0.0).astype(jnp.bfloat16)
             if t == 0:
                 ys[h][c] = value
-                if (c + 1) % PIECE == 0:
-                    send_next(h, c // PIECE)
             else:
                 out_ref[0, h * part:(h + 1) * part, c * TILE:(c + 1) * TILE] = value
 
@@ -206,35 +207,36 @@
     plan[...] = order(rows_ref[...][None, :], cols_ref[...][None, :], count_ref[0])
     plan_copy = pltpu.make_async_copy(plan, plan_ref, psem)
     plan_copy.start()
-    ahead = PIECES
-    first = gather_steps(0)
-    for run in first[:ahead]:
+    for run in gather_steps(0):
         run()
     own(1)
-    for run in first[ahead:]:
-        run()
     settle(0, 0)
     plan_copy.wait()
     for c in wcopies:
         c.wait()
-    second = gather_steps(1)
-    half = ahead // 2
-    layer(0, 0, {1: second[:half], 2: second[half:ahead]})
-    for run in second[ahead:]:
+    layer(0, 0, {})
+    push(0, 0)
+    for run in gather_steps(1):
         run()
+    push(0, 1)
     settle(0, 1)
-    layer(0, 1, {})
-    for run in pass_steps(0):
-        run()
+    pass_step(0, 0, 0)()
+    layer(0, 1, {2: [pass_step(0, ZN, 0)]})
+    push(1, 0)
+    for rel, k in ((0, 1), (XN, 0), (XN + ZN, 0), (ZN, 1), (XN, 1)):
+        pass_step(0, rel, k)()
+    push(1, 1)
+    pass_step(1, 0, 0)()
+    pass_step(0, XN + ZN, 1)()
     settle(1, 0)
-    final = pass_steps(1)
-    layer(1, 0, {i: final[i:i + 1] for i in range(4)})
-    for run in final[4:]:
-        run()
+    layer(1, 0, {1: [pass_step(1, ZN, 0)]})
+    for rel, k in ((XN, 0), (0, 1), (XN + ZN, 0), (ZN, 1), (XN, 1), (XN + ZN, 1)):
+        pass_step(1, rel, k)()
     settle(1, 1)
     layer(1, 1, {})
     for copy in sent:
-        copy.wait_send()
+        if not any(copy is c for c in pushed[:-1]):
+            copy.wait_send()
 
 
 def on_device(peers, held, tile_values, tile_rows, tile_cols, tile_count, bias):

time: 80.6 us -> 68.9 us (0.85)
  Pallas kernels: 77.9 us -> 66.2 us
    pallas_call x1, Pallas kernels: 77.9 us -> 66.2 us  [on_device(): pl.pallas_call(functools.partial(kernel, peers), out_shape=jax.ShapeDtype...]
where the time goes in v4:
time: 68.9 us; the launch traced here: 68.7 us
  Pallas kernels  66.2 us (96%)
  local copies, waits for them, and re-layouts  1.87 us (3%)
    pallas_call x1, Pallas kernels, on_device(): pl.pallas_call(functools.partial(kernel, peers), out_shape=jax.ShapeDtype...  66.2 us
    unnamed x1, local copies, waits for them, and re-layouts  1.87 us

profile of v4, /device:TPU:1, one launch (start us, length us, event | category | flops | bytes accessed | tf_op | source)
XLA Modules:
  0.0 68.7 jit_solution(1958615193067394036)
XLA Ops:
  0.7 66.2 %shard_map.64 = bf16[1,64,4096]{2,1,0:T(8,128)(2,1)} custom-call(s32[1]{0:T(128)S(6)} %copy.8.count_ref, s32[288]{0:T(512)} %rows_ref.1, s32[288]{0:T(512)} %cols_ref.1, bf16[1,64,4096]{2,1,0:T(8,128)(2,1)} %held_ref.1, bf16[288,128,128]{2,1,0:T(8,128)(2,1)} %w_hbm.1, f32[32,128]{1,0:T(8,128)} %bitcast.1), custom_call_target="tpu_custom_call" | custom-call | tf_op jit(solution)/shard_map/pallas_call | solution.py:251
  66.9 1.9 %copy.9 = bf16[1,64,4096]{2,1,0:T(8,128)(2,1)} copy(bf16[1,64,4096]{2,1,0:T(8,128)(2,1)} %shard_map.64) | data formatting | bytes 1048576

commit v5 on v4

--- a/solution.py
+++ b/solution.py
@@ -10,14 +10,14 @@
 TILE = 128
 SPLIT = 8
 COLT = 32
-HALVES = 2
+PARTS = 3
 PIECES = 2
 PIECE = COLT // PIECES
 GROUP = 40
 LANES = 384
 WPARTS = 4
 SIB, XN, ZN = 1, 2, 4
-N_SENDS = HALVES * PIECES * (7 + 8)
+N_SENDS = PARTS * PIECES * (7 + 8)
 
 
 def order(rows, cols, count):
@@ -65,12 +65,13 @@
 
 
 def kernel(peers, count_ref, rows_ref, cols_ref, held_ref, w_hbm, bias_ref, out_ref,
-           xa0, xa1, xb0, xb1, y0, y1, w, buf, plan, plan_ref, wsem, psem, send_sem, recv_sem):
-    xs = ((xa0, xa1), (xb0, xb1))
-    ys = (y0, y1)
+           xa0, xa1, xa2, xb0, xb1, xb2, y0, y1, y2, w, buf, plan, plan_ref, wsem, psem, send_sem, recv_sem):
+    xs = ((xa0, xa1, xa2), (xb0, xb1, xb2))
+    ys = (y0, y1, y2)
     slots = rows_ref.shape[0]
     pairs = (slots + COLT) // 2
-    part = held_ref.shape[1] // HALVES
+    batch = held_ref.shape[1]
+    starts = (0, batch // 4, batch * 3 // 4, batch)
     me = lax.axis_index("section")
     place = me % SPLIT
     base = me - place
@@ -102,9 +103,9 @@
         pl.semaphore_signal(barrier, inc=1, device_id={"section": dev},
                             device_id_type=pl.DeviceIdType.MESH)
 
-    for h in range(HALVES):
+    for h in range(PARTS):
         for c in range(COLT):
-            xs[0][h][place * COLT + c] = held_ref[0, h * part:(h + 1) * part, c * TILE:(c + 1) * TILE]
+            xs[0][h][place * COLT + c] = held_ref[0, starts[h]:starts[h + 1], c * TILE:(c + 1) * TILE]
     buf[pairs] = jnp.zeros(buf.shape[1:], buf.dtype)
     for x in xs[0] + xs[1]:
         x[SPLIT * COLT] = jnp.zeros(x.shape[1:], x.dtype)
@@ -177,63 +178,84 @@
             for k in range(PIECES):
                 arrive(t, h, rel, k)
 
-    def tiles(x, low, high, total):
-        def body(i, total):
-            for j in range(GROUP):
-                pair = i * GROUP + j
-                a, b = 2 * pair, 2 * pair + 1
-                left = jnp.concatenate([x[plan_ref[1, a]], x[plan_ref[1, b]]], axis=1)
-                right = jnp.concatenate([w[plan_ref[0, a]], w[plan_ref[0, b]]], axis=0)
-                product = jnp.dot(left, right, preferred_element_type=jnp.float32)
-                total = jnp.where(plan_ref[2, a] == 1, product, total + product)
-                buf[pair] = total
-            return total
-        return lax.fori_loop(low, high, body, total)
-
-    def layer(t, h, between):
-        total = jnp.zeros(buf.shape[1:], buf.dtype)
+    def tiles(inputs, i, total):
+        rows = total.shape[0]
+
+        def tile(at):
+            return jnp.concatenate([x[at] for x in inputs], axis=0)
+
+        for j in range(GROUP):
+            pair = i * GROUP + j
+            a, b = 2 * pair, 2 * pair + 1
+            left = jnp.concatenate([tile(plan_ref[1, a]), tile(plan_ref[1, b])], axis=1)
+            right = jnp.concatenate([w[plan_ref[0, a]], w[plan_ref[0, b]]], axis=0)
+            product = jnp.dot(left, right, preferred_element_type=jnp.float32)
+            total = jnp.where(plan_ref[2, a] == 1, product, total + product)
+            buf[pair, :rows] = total
+        return total
+
+    def layer(inputs, put, between):
+        rows = sum(x.shape[1] for x in inputs)
+        total = jnp.zeros((rows, TILE), buf.dtype)
         for i in range(pairs // GROUP):
-            total = tiles(xs[t][h], i, i + 1, total)
+            total = tiles(inputs, i, total)
             for run in between.get(i, ()):
                 run()
         for c in range(COLT):
-            value = jnp.maximum(buf[plan_ref[3, c]] + bias_ref[c:c + 1, :], 0.0).astype(jnp.bfloat16)
-            if t == 0:
-                ys[h][c] = value
-            else:
-                out_ref[0, h * part:(h + 1) * part, c * TILE:(c + 1) * TILE] = value
+            value = buf[plan_ref[3, c], :rows] + bias_ref[c:c + 1, :]
+            put(c, jnp.maximum(value, 0.0).astype(jnp.bfloat16))
+
+    def tick(h, between):
+        def put(c, value):
+            ys[h][c] = value
+        layer(xs[0][h:h + 1], put, between)
+
+    def put_out(c, value):
+        out_ref[0, :, c * TILE:(c + 1) * TILE] = value
 
     own(0)
     plan[...] = order(rows_ref[...][None, :], cols_ref[...][None, :], count_ref[0])
     plan_copy = pltpu.make_async_copy(plan, plan_ref, psem)
     plan_copy.start()
-    for run in gather_steps(0):
-        run()
+    def run_all(steps):
+        for run in steps:
+            run()
+
+    second, third = gather_steps(1), gather_steps(2)
+    run_all(gather_steps(0))
     own(1)
     settle(0, 0)
     plan_copy.wait()
     for c in wcopies:
         c.wait()
-    layer(0, 0, {})
+    tick(0, {})
     push(0, 0)
-    for run in gather_steps(1):
-        run()
+    run_all(second[:4])
     push(0, 1)
+    run_all(second[4:])
+    own(2)
     settle(0, 1)
     pass_step(0, 0, 0)()
-    layer(0, 1, {2: [pass_step(0, ZN, 0)]})
+    pass_step(0, 0, 1)()
+    tick(1, {1: third[:4], 2: [pass_step(0, ZN, 0), pass_step(0, ZN, 1)]})
     push(1, 0)
-    for rel, k in ((0, 1), (XN, 0), (XN + ZN, 0), (ZN, 1), (XN, 1)):
+    run_all(third[4:])
+    settle(0, 2)
+    for rel, k in ((XN, 0), (XN, 1), (XN + ZN, 0), (XN + ZN, 1)):
         pass_step(0, rel, k)()
-    push(1, 1)
-    pass_step(1, 0, 0)()
-    pass_step(0, XN + ZN, 1)()
-    settle(1, 0)
-    layer(1, 0, {1: [pass_step(1, ZN, 0)]})
-    for rel, k in ((XN, 0), (0, 1), (XN + ZN, 0), (ZN, 1), (XN, 1), (XN + ZN, 1)):
-        pass_step(1, rel, k)()
-    settle(1, 1)
-    layer(1, 1, {})
+    tick(2, {2: [lambda: push(1, 1)], 3: [pass_step(1, 0, 0)]})
+    pass_step(1, ZN, 0)()
+    pass_step(1, XN, 0)()
+    push(2, 0)
+    for h, rel, k in ((1, XN + ZN, 0), (1, 0, 1)):
+        pass_step(h, rel, k)()
+    push(2, 1)
+    for h, rel, k in ((2, 0, 0), (1, ZN, 1), (1, XN, 1), (2, ZN, 0), (2, XN, 0), (2, 0, 1), (1, XN + ZN, 1),
+                      (2, ZN, 1), (2, XN + ZN, 0), (2, XN, 1), (2, XN + ZN, 1)):
+        pass_step(h, rel, k)()
+    for h in range(PARTS):
+        settle(1, h)
+    layer(xs[1], put_out, {})
     for copy in sent:
         if not any(copy is c for c in pushed[:-1]):
             copy.wait_send()
@@ -242,27 +264,27 @@
 def on_device(peers, held, tile_values, tile_rows, tile_cols, tile_count, bias):
     slots = tile_rows.shape[0]
     batch = held.shape[1]
-    part = batch // HALVES
+    sizes = (batch // 4, batch // 2, batch // 4)
     pairs = (slots + COLT) // 2
     smem = pl.BlockSpec(memory_space=pltpu.SMEM)
     vmem = pl.BlockSpec(memory_space=pltpu.VMEM)
-    x = pltpu.VMEM((SPLIT * COLT + 1, part, TILE), jnp.bfloat16)
-    y = pltpu.VMEM((COLT, part, TILE), jnp.bfloat16)
+    xs = [pltpu.VMEM((SPLIT * COLT + 1, size, TILE), jnp.bfloat16) for size in sizes]
+    ys = [pltpu.VMEM((COLT, size, TILE), jnp.bfloat16) for size in sizes]
     return pl.pallas_call(
         functools.partial(kernel, peers),
         out_shape=jax.ShapeDtypeStruct(held.shape, jnp.bfloat16),
         in_specs=[smem, vmem, vmem, vmem, pl.BlockSpec(memory_space=pl.ANY), vmem],
         out_specs=vmem,
         scratch_shapes=[
-            x, x, x, x, y, y,
+            *xs, *xs, *ys,
             pltpu.VMEM((slots, TILE, TILE), jnp.bfloat16),
-            pltpu.VMEM((pairs + 1, part, TILE), jnp.float32),
+            pltpu.VMEM((pairs + 1, batch, TILE), jnp.float32),
             pltpu.VMEM((8, LANES), jnp.int32),
             pltpu.SMEM((8, LANES), jnp.int32),
             pltpu.SemaphoreType.DMA((WPARTS,)),
             pltpu.SemaphoreType.DMA,
             pltpu.SemaphoreType.DMA((N_SENDS,)),
-            pltpu.SemaphoreType.DMA((2, HALVES, SPLIT, PIECES)),
+            pltpu.SemaphoreType.DMA((2, PARTS, SPLIT, PIECES)),
         ],
         compiler_params=pltpu.CompilerParams(
             collective_id=0, has_side_effects=True, vmem_limit_bytes=56 * 1024 * 1024),

time: 68.9 us -> 71.7 us (1.041)
  Pallas kernels: 66.2 us -> 69 us
    pallas_call x1, Pallas kernels: 66.2 us -> 69 us  [on_device(): pl.pallas_call(functools.partial(kernel, peers), out_shape=jax.ShapeDtype...]
where the time goes in v5:
time: 71.7 us; the launch traced here: 71.6 us
  Pallas kernels  69 us (96%)
  local copies, waits for them, and re-layouts  1.87 us (3%)
    pallas_call x1, Pallas kernels, on_device(): pl.pallas_call(functools.partial(kernel, peers), out_shape=jax.ShapeDtype...  69 us
    unnamed x1, local copies, waits for them, and re-layouts  1.87 us

profile of v5, /device:TPU:1, one launch (start us, length us, event | category | flops | bytes accessed | tf_op | source)
XLA Modules:
  0.0 71.6 jit_solution(1420837827904247264)
XLA Ops:
  0.7 69.0 %shard_map.64 = bf16[1,64,4096]{2,1,0:T(8,128)(2,1)} custom-call(s32[1]{0:T(128)S(6)} %copy.8.count_ref, s32[288]{0:T(512)} %rows_ref.1, s32[288]{0:T(512)} %cols_ref.1, bf16[1,64,4096]{2,1,0:T(8,128)(2,1)} %held_ref.1, bf16[288,128,128]{2,1,0:T(8,128)(2,1)} %w_hbm.1, f32[32,128]{1,0:T(8,128)} %bitcast.1), custom_call_target="tpu_custom_call" | custom-call | tf_op jit(solution)/shard_map/pallas_call | solution.py:273
  69.7 1.9 %copy.9 = bf16[1,64,4096]{2,1,0:T(8,128)(2,1)} copy(bf16[1,64,4096]{2,1,0:T(8,128)(2,1)} %shard_map.64) | data formatting | bytes 1048576

commit v6 on v4

--- a/solution.py
+++ b/solution.py
@@ -221,17 +221,21 @@
     push(0, 1)
     settle(0, 1)
     pass_step(0, 0, 0)()
-    layer(0, 1, {2: [pass_step(0, ZN, 0)]})
+    layer(0, 1, {1: [pass_step(0, ZN, 0)], 3: [pass_step(0, 0, 1)]})
     push(1, 0)
-    for rel, k in ((0, 1), (XN, 0), (XN + ZN, 0), (ZN, 1), (XN, 1)):
+    for rel, k in ((XN, 0), (XN + ZN, 0), (ZN, 1), (XN, 1)):
         pass_step(0, rel, k)()
     push(1, 1)
     pass_step(1, 0, 0)()
     pass_step(0, XN + ZN, 1)()
     settle(1, 0)
-    layer(1, 0, {1: [pass_step(1, ZN, 0)]})
-    for rel, k in ((XN, 0), (0, 1), (XN + ZN, 0), (ZN, 1), (XN, 1), (XN + ZN, 1)):
-        pass_step(1, rel, k)()
+    layer(1, 0, {
+        0: [pass_step(1, ZN, 0)],
+        1: [pass_step(1, XN, 0), pass_step(1, 0, 1)],
+        2: [pass_step(1, XN + ZN, 0), pass_step(1, ZN, 1)],
+        3: [pass_step(1, XN, 1)],
+    })
+    pass_step(1, XN + ZN, 1)()
     settle(1, 1)
     layer(1, 1, {})
     for copy in sent:

time: 68.9 us -> 67.8 us (0.984)
  Pallas kernels: 66.2 us -> 65.1 us
    pallas_call x1, Pallas kernels: 66.2 us -> 65.1 us  [on_device(): pl.pallas_call(functools.partial(kernel, peers), out_shape=jax.ShapeDtype...]
where the time goes in v6:
time: 67.8 us; the launch traced here: 67.6 us
  Pallas kernels  65.1 us (96%)
  local copies, waits for them, and re-layouts  1.87 us (3%)
    pallas_call x1, Pallas kernels, on_device(): pl.pallas_call(functools.partial(kernel, peers), out_shape=jax.ShapeDtype...  65.1 us
    unnamed x1, local copies, waits for them, and re-layouts  1.87 us

profile of v6, /device:TPU:1, one launch (start us, length us, event | category | flops | bytes accessed | tf_op | source)
XLA Modules:
  0.0 67.6 jit_solution(14436425572967042705)
XLA Ops:
  0.7 65.1 %shard_map.64 = bf16[1,64,4096]{2,1,0:T(8,128)(2,1)} custom-call(s32[1]{0:T(128)S(6)} %copy.8.count_ref, s32[288]{0:T(512)} %rows_ref.1, s32[288]{0:T(512)} %cols_ref.1, bf16[1,64,4096]{2,1,0:T(8,128)(2,1)} %held_ref.1, bf16[288,128,128]{2,1,0:T(8,128)(2,1)} %w_hbm.1, f32[32,128]{1,0:T(8,128)} %bitcast.1), custom_call_target="tpu_custom_call" | custom-call | tf_op jit(solution)/shard_map/pallas_call | solution.py:255
  65.8 1.9 %copy.9 = bf16[1,64,4096]{2,1,0:T(8,128)(2,1)} copy(bf16[1,64,4096]{2,1,0:T(8,128)(2,1)} %shard_map.64) | data formatting | bytes 1048576
